TPU v7x, 256 devices: a whole 4x4x8 slice. The times are simulated.
256 devices in a mesh: feat: 8 (over z_hi, y), node: 32 (over x, z_lo, core).
Axes of the slice: x: 4, y: 4, z: 8 (z_hi: 2, z_lo: 4; z = z_hi * 4 + z_lo), core: 2. Of those that a mesh axis runs over, the one named last changes fastest.
Arguments:
- features: bfloat16 [65536, 4096], P('node', 'feat'), may hold values from -6 to 6
- seed_feats: bfloat16 [4096, 4096], P('node', 'feat'), may hold values from -6 to 6
- patterns: int32 [1024, 8, 128, 8], P('node'), may hold values from 0 to 65535, as said below
- sources: int32 [1024, 8], P('node'), may hold values from 0 to 15
- counts: int32 [1024], P('node'), may hold values from 1 to 8
- w_self: bfloat16 [4096, 1024], P('feat'), may hold values from -0.09375 to 0.09375
- w_neigh: bfloat16 [4096, 1024], P('feat'), may hold values from -0.09375 to 0.09375
- bias_term: float32 [1024], replicated, may hold values from -3 to 3
- out_grad: bfloat16 [4096, 1024], P('node'), may hold values from -0.3125 to 0.3125
Outputs:
- hidden: bfloat16 [4096, 1024], P('node')
- grad_self: float32 [4096, 1024], P(('feat', 'node'))
- grad_neigh: float32 [4096, 1024], P(('feat', 'node'))
- grad_bias: float32 [1024], P('node')
Inputs may be any that keep to these rules, and one draw needn't show every extreme that they name: `patterns`: each word holds 16 entries of 0 or 1 in its 16 low bits.
All inputs are finite; a program needn't handle non-finite values.
Results may differ from a plain program's by a relative error of at most 0.024.
The roundings to bfloat16 on the way count: a program that leaves them out, or rounds other values in their place, can miss the bound.
Values may be sent and summed in bfloat16 or wider, within the bound.
No kernel may reach another device: no remote copies, remote signals or barrier semaphores. Data moves between devices by JAX's collectives and lax.ppermute only.
A program may use at most 128 MiB of HBM per device.

v0:
```python
import jax
import jax.numpy as jnp
from jax import lax
from jax.sharding import PartitionSpec as P


def unpack(packed):
    shifts = jnp.arange(16, dtype=jnp.int32)
    bit_values = jnp.bitwise_and(jnp.right_shift(packed[..., None], shifts), 1)
    return bit_values.reshape(packed.shape[:-1] + (packed.shape[-1] * 16,)).astype(jnp.bfloat16)


def body(features, seed_feats, patterns, sources, counts, w_self, w_neigh, bias_term, out_grad):
    targets = patterns.shape[0]
    fan_slots = patterns.shape[1]
    block_rows = patterns.shape[2]
    local_blocks = features.shape[0] // block_rows
    live_mask = jnp.arange(fan_slots, dtype=jnp.int32)[None, :] < counts[:, None]
    tile_bits = unpack(patterns) * live_mask[:, :, None, None].astype(jnp.bfloat16)
    source_pick = (
        sources[:, :, None] == jnp.arange(local_blocks, dtype=jnp.int32)[None, None, :]
    ).astype(jnp.bfloat16)
    mixing = jnp.einsum(
        "tkrs,tkb->trbs", tile_bits, source_pick, preferred_element_type=jnp.bfloat16
    )
    mixing = mixing.reshape(targets * block_rows, local_blocks * block_rows)
    summed_rows = jnp.dot(mixing, features, preferred_element_type=jnp.float32)
    degree = jnp.sum(mixing, axis=1, dtype=jnp.float32)
    owner_sums, owner_counts = (
        lax.psum_scatter(summed_rows, "node", scatter_dimension=0, tiled=True),
        lax.psum_scatter(degree, "node", scatter_dimension=0, tiled=True),
    )
    aggregate = (owner_sums / jnp.sqrt(1.0 + owner_counts)[:, None]).astype(jnp.bfloat16)
    local_pre = jnp.dot(seed_feats, w_self, preferred_element_type=jnp.float32)
    local_pre = local_pre + jnp.dot(aggregate, w_neigh, preferred_element_type=jnp.float32)
    pre_act = lax.psum(local_pre, "feat")
    hidden = jnp.maximum(pre_act + bias_term, 0.0).astype(jnp.bfloat16)
    grad_rows = jnp.where(hidden > 0, out_grad, jnp.zeros_like(out_grad))
    contract_rows = (((0,), (0,)), ((), ()))
    grad_self = lax.dot_general(
        seed_feats, grad_rows, contract_rows, preferred_element_type=jnp.float32
    )
    grad_neigh = lax.dot_general(
        aggregate, grad_rows, contract_rows, preferred_element_type=jnp.float32
    )
    grad_bias = jnp.sum(grad_rows.astype(jnp.float32), axis=0)
    grad_self, grad_neigh, grad_bias = (
        lax.psum_scatter(grad_self, "node", scatter_dimension=0, tiled=True),
        lax.psum_scatter(grad_neigh, "node", scatter_dimension=0, tiled=True),
        lax.psum_scatter(grad_bias, "node", scatter_dimension=0, tiled=True),
    )
    return (hidden, grad_self, grad_neigh, grad_bias)


def solution(mesh):
    return jax.shard_map(
        body,
        mesh=mesh,
        in_specs=(
            P("node", "feat"),
            P("node", "feat"),
            P("node", None, None, None),
            P("node", None),
            P("node"),
            P("feat", None),
            P("feat", None),
            P(),
            P("node", None),
        ),
        out_specs=(
            P("node", None),
            P(("feat", "node"), None),
            P(("feat", "node"), None),
            P("node"),
        ),
        check_vma=False,
    )
```

profile of v0, /device:TPU:16, one launch (start us, length us, event | category | flops | bytes accessed | tf_op | source)
XLA Modules:
  0.0 658.3 jit_solution(8293639627767520409)
XLA Ops:
  7.2 0.0 copy-start
  7.2 0.0 reduce-scatter.6.cloned.1.call-start
  7.2 0.9 fusion.10
  8.1 0.1 shift_right_arithmetic.23
  8.2 9.6 %fusion.5 = bf16[32,8,128,128]{2,3,1,0:T(8,128)(2,1)} fusion(s32[128]{0:T(128)S(1)} %shift_right_arithmetic.23, s32[32,8,128,8]{2,3,1,0:T(8,128)} %param.11, bf16[32,8]{1,0:T(8,128)(2,1)S(1)} %fusion.10), kind=kLoop, calls=%fused_computation.7 | loop fusion | flops 29360128 | bytes 9438208 | tf_op jit(solution)/shard_map/mul | solution.py:19
  17.8 0.0 copy-start.5
  17.8 12.4 %copy.20 = bf16[32,8,128,128]{3,1,2,0:T(8,128)(2,1)} copy(bf16[32,8,128,128]{2,3,1,0:T(8,128)(2,1)} %fusion.5) | data formatting | bytes 16777216 | tf_op jit(solution)/shard_map/mul | solution.py:19
  30.2 0.0 copy-done.5
  30.2 0.1 copy.19
  30.2 39.7 %convert_reduce_fusion = (f32[32,128]{1,0:T(8,128)S(1)}, bf16[32,16,128,128]{3,1,2,0:T(8,128)(2,1)}) fusion(bf16[32,8,128,128]{3,1,2,0:T(8,128)(2,1)} %copy.20, s32[32,8]{1,0:T(8,128)S(1)} %copy.19), kind=kOutput, calls=%fused_computation | convolution fusion | flops 150994944 | bytes 25183232 | tf_op jit(solution)/shard_map/tkrs,tkb->trbs/dot_general | solution.py:23
  70.0 0.0 copy-done
  70.0 14.4 %fusion = f32[4096,512]{1,0:T(8,128)} fusion(bf16[2048,512]{1,0:T(8,128)(2,1)S(1)} %copy-done, bf16[512,8,16,128]{3,2,1,0:T(8,128)(2,1)} %bitcast.33), kind=kOutput, calls=%fused_computation.1 | convolution fusion | flops 8589934592 | bytes 27262976 | tf_op jit(solution)/shard_map/dot_general | solution.py:27
  84.4 0.0 copy-start.6
  84.4 0.0 copy-start.3
  84.4 0.0 copy-start.1
  84.4 0.0 copy-start.4
  84.4 0.0 reduce-scatter.6.cloned.1.call-update
  84.4 0.0 all-reduce.4.cloned.1.call-start
  84.5 0.6 copy-done.6
  85.1 0.6 dynamic-slice
  86.3 140.5 %all-reduce = f32[4096]{0:T(1024)S(1)} all-reduce(f32[4096]{0:T(1024)S(1)} %bitcast.34), channel_id=3, replica_groups=mesh['feat'=8,'node'=32] {'node'}, use_global_device_ids=true, to_apply=%region_2.0.clone | all-reduce | flops 4096 | bytes 32768
  226.8 0.1 fusion.11
  226.9 0.0 copy-done.3
  226.9 1.5 fusion.13
  228.5 21.3 %reduce-scatter.6.cloned.1.call-done = f32[128,512]{1,0:T(8,128)} async-done(((f32[4096,512]{1,0:T(8,128)}), f32[128,512]{1,0:T(8,128)}) %reduce-scatter.6.cloned.1.call-update) | async-done | bytes 262160 | tf_op jit(solution)/shard_map/reduce_scatter | solution.py:30
  249.7 2.5 convolution_add_fusion
  252.2 0.0 all-reduce.4.cloned.1.call-update
  252.2 0.0 reduce-scatter.8.cloned.1.call-start
  252.3 99.6 %all-reduce.4.cloned.1.call-done = f32[128,1024]{1,0:T(8,128)} async-done(((f32[128,1024]{1,0:T(8,128)}), f32[128,1024]{1,0:T(8,128)}) %all-reduce.4.cloned.1.call-update) | async-done | bytes 524304 | tf_op jit(solution)/shard_map/psum | solution.py:36
  351.9 0.0 copy-done.1
  351.9 0.0 copy-done.4
  351.9 1.2 convert_reduce_fusion.1
  353.0 0.0 copy-start.2
  353.1 2.9 fusion.12
  356.0 0.0 reduce-scatter.8.cloned.1.call-update
  356.0 0.0 reduce-scatter.10.cloned.1.call-start
  356.1 1.8 convolution_bitcast_fusion
  357.9 2.9 copy.23
  360.7 0.0 reduce-scatter.10.cloned.1.call-update
  361.4 67.8 %all-reduce.1 = f32[1024]{0:T(1024)S(1)} all-reduce(f32[1024]{0:T(1024)S(1)} %get-tuple-element.16), channel_id=6, replica_groups=mesh['feat'=8,'node'=32] {'node'}, use_global_device_ids=true, to_apply=%region_7.8.clone | all-reduce | flops 1024 | bytes 8192
  429.2 0.6 dynamic-slice.3
  429.8 75.0 %reduce-scatter.8.cloned.1.call-done = f32[16,1024]{1,0:T(8,128)} async-done(((f32[512,1024]{1,0:T(8,128)}), f32[16,1024]{1,0:T(8,128)}) %reduce-scatter.8.cloned.1.call-update) | async-done | bytes 65552 | tf_op jit(solution)/shard_map/reduce_scatter | solution.py:49
  504.7 147.0 %reduce-scatter.10.cloned.1.call-done = f32[16,1024]{1,0:T(8,128)} async-done(((f32[512,1024]{1,0:T(8,128)}), f32[16,1024]{1,0:T(8,128)}) %reduce-scatter.10.cloned.1.call-update) | async-done | bytes 65552
  651.8 0.0 copy-done.2
  (1 shorter events, 0.0 us)
Async XLA Ops:
  7.2 62.8 %copy-start = (bf16[2048,512]{1,0:T(8,128)(2,1)S(1)}, bf16[2048,512]{1,0:T(8,128)(2,1)}, u32[]{:S(2)}) copy-start(bf16[2048,512]{1,0:T(8,128)(2,1)} %param.9) | copy-start | bytes 6291460
  7.2 242.6 %reduce-scatter.6.cloned.1.call-start = ((), (), s32[]{:S(2)}) async-start(), calls=%async_computation.3 | async-start | bytes 8650752 | tf_op jit(solution)/shard_map/reduce_scatter | solution.py:30
  17.8 12.4 %copy-start.5 = (s32[32,8]{0,1:T(8,128)S(1)}, s32[32,8]{0,1:T(8,128)}, u32[]{:S(2)}) copy-start(s32[32,8]{0,1:T(8,128)} %param.12) | copy-start | bytes 3076
  84.4 0.7 copy-start.6
  84.4 142.5 %copy-start.3 = (bf16[128,512]{1,0:T(8,128)(2,1)S(1)}, bf16[128,512]{1,0:T(8,128)(2,1)}, u32[]{:S(2)}) copy-start(bf16[128,512]{1,0:T(8,128)(2,1)} %param.10) | copy-start | bytes 393220
  84.4 267.5 %copy-start.1 = (bf16[128,1024]{1,0:T(8,128)(2,1)S(1)}, bf16[128,1024]{1,0:T(8,128)(2,1)}, u32[]{:S(2)}) copy-start(bf16[128,1024]{1,0:T(8,128)(2,1)} %param.17) | copy-start | bytes 786436
  84.4 267.5 %copy-start.4 = (f32[1024]{0:T(1024)S(1)}, f32[1024]{0:T(1024)}, u32[]{:S(2)}) copy-start(f32[1024]{0:T(1024)} %param.16) | copy-start | bytes 12292
  84.4 267.4 %all-reduce.4.cloned.1.call-start = ((), (), s32[]{:S(2)}) async-start(), calls=%async_computation.4 | async-start | bytes 1048576 | tf_op jit(solution)/shard_map/psum | solution.py:36
  252.2 252.5 %reduce-scatter.8.cloned.1.call-start = ((), (), s32[]{:S(2)}) async-start(), calls=%async_computation.5 | async-start | bytes 2162688 | tf_op jit(solution)/shard_map/reduce_scatter | solution.py:49
  353.0 298.7 %copy-start.2 = (bf16[128,1024]{1,0:T(8,128)(2,1)}, bf16[128,1024]{1,0:T(8,128)(2,1)S(1)}, u32[]{:S(2)}) copy-start(bf16[128,1024]{1,0:T(8,128)(2,1)S(1)} %get-tuple-element.17) | copy-start | bytes 786436
  356.0 295.7 %reduce-scatter.10.cloned.1.call-start = ((), (), s32[]{:S(2)}) async-start(), calls=%async_computation.6 | async-start | bytes 2162688
Sparse Core Ops, SparseCore 0:
  84.6 165.1 reduce-scatter.5
  252.4 99.4 all-reduce.3
  356.1 148.5 reduce-scatter.7
  507.7 144.0 reduce-scatter.9
where the time goes:
time: 659 us; the launch traced here: 658 us
  waiting for transfers between devices  343 us (52%)
  blocking collectives  208 us (32%)
  matrix products  62.9 us (10%)
  local copies, waits for them, and re-layouts  17.2 us (3%)
  between operations  15.1 us (2%)
  other arithmetic  11.7 us (2%)
    unnamed x2, blocking collectives  208 us
    unnamed x5, waiting for transfers between devices  147 us
    psum x1, waiting for transfers between devices, body(): pre_act = lax.psum(local_pre, 'feat')  99.6 us
    reduce_scatter x1, waiting for transfers between devices, body(): lax.psum_scatter(grad_neigh, 'node', scatter_dimension=0, tiled=True)  75 us
    dot_general x1, matrix products, body(): jnp.einsum('tkrs,tkb->trbs', tile_bits, source_pick, preferred_element_ty...  39.7 us
    reduce_scatter x1, waiting for transfers between devices, body(): lax.psum_scatter(summed_rows, 'node', scatter_dimension=0, tiled=True)  21.3 us
    dot_general x1, matrix products, body(): summed_rows = jnp.dot(mixing, features, preferred_element_type=jnp.float32)  14.4 us
  transfers between devices with their start and end apart: 4, of which 4 were waited for; matrix products, arithmetic and copies ran while one was open for 1% of the time, Pallas kernels for 0%

commit v1 on v0

v1 whole, which is shorter than its diff:
```python
import functools

import jax
import jax.numpy as jnp
from jax import lax
from jax.experimental import pallas as pl
from jax.experimental.pallas import tpu as pltpu
from jax.sharding import PartitionSpec as P

BLK = 128
HALF = 256
FAN = 8
TOP = 32700.0
NX, NZ, NY = 4, 4, 4
VMEM = pl.BlockSpec(memory_space=pltpu.VMEM)
SMEM = pl.BlockSpec(memory_space=pltpu.SMEM)
PARAMS = pltpu.CompilerParams(vmem_limit_bytes=48 * 1024 * 1024)


def node_of(x, z, c):
    return x * (NZ * 2) + z * 2 + c


def shift_x(d):
    return [
        (node_of(x, z, c), node_of((x + d) % NX, z, c))
        for x in range(NX) for z in range(NZ) for c in range(2)
    ]


def shift_z(d):
    return [
        (node_of(x, z, c), node_of(x, (z + d) % NZ, c))
        for x in range(NX) for z in range(NZ) for c in range(2)
    ]


SWAP_CORE = [(n, n ^ 1) for n in range(NX * NZ * 2)]
SWAP_FAR = [(f, f ^ 4) for f in range(8)]


def shift_y(d):
    return [(h * 4 + y, h * 4 + (y + d) % NY) for h in range(2) for y in range(NY)]


def split_kernel(core_ref, feat_ref, seed_ref, mine_ref, theirs_ref, smine_ref, stheirs_ref, turned, sturned):
    core = core_ref[0]
    turned[...] = feat_ref[...].T

    @pl.when(pl.program_id(0) == 0)
    def _():
        sturned[...] = seed_ref[...].T

    for block in range(16):
        keep = pl.ds(pl.multiple_of(block * 32 + core * 16, 16), 16)
        give = pl.ds(pl.multiple_of(block * 32 + (1 - core) * 16, 16), 16)
        rows = pl.ds(block * 16, 16)
        mine_ref[rows, :] = turned[keep, :]
        theirs_ref[rows, :] = turned[give, :]

        @pl.when(pl.program_id(0) == 0)
        def _():
            smine_ref[rows, :] = sturned[keep, :]
            stheirs_ref[rows, :] = sturned[give, :]


def split(core, features, seed_feats):
    nodes = features.shape[0]
    step = 512
    half = jax.ShapeDtypeStruct((HALF, nodes), jnp.bfloat16)
    shalf = jax.ShapeDtypeStruct((HALF, BLK), jnp.bfloat16)
    cols = pl.BlockSpec((HALF, step), lambda i, s: (0, i))
    whole = pl.BlockSpec((HALF, BLK), lambda i, s: (0, 0))
    return pl.pallas_call(
        split_kernel,
        out_shape=(half, half, shalf, shalf),
        grid_spec=pltpu.PrefetchScalarGridSpec(
            num_scalar_prefetch=1,
            grid=(nodes // step,),
            in_specs=[
                pl.BlockSpec((step, 512), lambda i, s: (i, 0)),
                pl.BlockSpec((BLK, 512), lambda i, s: (0, 0)),
            ],
            out_specs=[cols, cols, whole, whole],
            scratch_shapes=[pltpu.VMEM((512, step), jnp.bfloat16), pltpu.VMEM((512, BLK), jnp.bfloat16)],
        ),
        compiler_params=PARAMS,
        name="split",
    )(core, features, seed_feats)


def step_of(mantissa, exponent):
    return mantissa * jnp.exp2(exponent)


def encode(sums, count):
    top = jnp.maximum(jnp.max(jnp.abs(sums), axis=0, keepdims=True), 1e-25) * (1.0 / TOP)
    exponent = jnp.floor(jnp.log2(top)) - 13.0
    mantissa = jnp.ceil(top * jnp.exp2(-exponent))
    coded = jnp.round(sums * (1.0 / step_of(mantissa, exponent))).astype(jnp.int32).astype(jnp.int16)
    row = lax.broadcasted_iota(jnp.int32, (16, BLK), 0)
    tail = jnp.where(row == 0, count, jnp.where(row == 1, exponent, jnp.where(row == 2, mantissa, 0.0)))
    return coded, tail.astype(jnp.int32).astype(jnp.int16)


def decode(ref, index):
    tail = ref[index, pl.ds(HALF, 16), :].astype(jnp.int32).astype(jnp.float32)
    values = ref[index, pl.ds(0, HALF), :].astype(jnp.int32).astype(jnp.float32)
    return values * step_of(tail[2:3], tail[1:2]), tail[0:1]


def sums_kernel(coded_out, meta_ref, pat0_ref, pat1_ref, feat0_ref, feat1_ref, out_ref, acc, pop):
    target = meta_ref[0] + pl.program_id(0)
    shifts = lax.broadcasted_iota(jnp.int32, (FAN, 16, BLK), 1)
    acc[...] = jnp.zeros_like(acc)
    pop[...] = jnp.zeros_like(pop)
    for side, (pat_ref, feat_ref) in enumerate(((pat0_ref, feat0_ref), (pat1_ref, feat1_ref))):
        live = meta_ref[1 + side * 32 + target]

        def group(first):
            tiles, picked = [], []
            for slot in range(first, first + 4):
                words = pat_ref[0, slot] * (slot < live).astype(jnp.int32)
                pop[...] += lax.population_count(words)
                bits = (jnp.broadcast_to(words[:, None, :], (FAN, 16, BLK)) >> shifts) & 1
                tiles.append(bits.reshape(BLK, BLK).astype(jnp.float32).astype(jnp.bfloat16))
                source = meta_ref[65 + (side * 32 + target) * FAN + slot]
                picked.append(feat_ref[:, pl.ds(pl.multiple_of(source * BLK, BLK), BLK)])
            acc[...] += jnp.dot(
                jnp.concatenate(picked, axis=1), jnp.concatenate(tiles, axis=0),
                preferred_element_type=jnp.float32,
            )

        group(0)
        pl.when(live > 4)(functools.partial(group, 4))
    count = jnp.sum(pop[...], axis=0, keepdims=True).astype(jnp.float32)
    if coded_out:
        coded, tail = encode(acc[...], count)
        out_ref[0, pl.ds(0, HALF), :] = coded
        out_ref[0, pl.ds(HALF, 16), :] = tail
    else:
        out_ref[0, pl.ds(0, HALF), :] = acc[...]
        out_ref[0, pl.ds(HALF, 8), :] = jnp.broadcast_to(count, (8, BLK))


def sums(coded_out, meta, pat0, pat1, feat0, feat1):
    nodes = feat0.shape[1]
    pats = pl.BlockSpec((1, FAN, 8, BLK), lambda i, m: (m[0] + i, 0, 0, 0))
    feats = pl.BlockSpec((HALF, nodes), lambda i, m: (0, 0))
    rows, kind = (HALF + 16, jnp.int16) if coded_out else (HALF + 8, jnp.float32)
    return pl.pallas_call(
        functools.partial(sums_kernel, coded_out),
        out_shape=jax.ShapeDtypeStruct((8, rows, BLK), kind),
        grid_spec=pltpu.PrefetchScalarGridSpec(
            num_scalar_prefetch=1,
            grid=(8,),
            in_specs=[pats, pats, feats, feats],
            out_specs=pl.BlockSpec((1, rows, BLK), lambda i, m: (i, 0, 0)),
            scratch_shapes=[pltpu.VMEM((HALF, BLK), jnp.float32), pltpu.VMEM((8, BLK), jnp.int32)],
        ),
        compiler_params=PARAMS,
        cost_estimate=pl.CostEstimate(flops=2_000_000_000, bytes_accessed=3_000_000, transcendentals=0),
        name="sums",
    )(meta, pat0, pat1, feat0, feat1)


def merge_x_kernel(pos_ref, r1_ref, r2_ref, r3_ref, own_ref, kept_ref, o1_ref, o2_ref, o3_ref):
    z = pos_ref[1]
    for d, out_ref in enumerate((kept_ref, o1_ref, o2_ref, o3_ref)):
        for c in range(2):
            index = lax.rem(z + d, NZ) * 2 + c
            total = own_ref[index, pl.ds(0, HALF), :]
            count = own_ref[index, pl.ds(HALF, 8), :][0:1]
            for ref in (r1_ref, r2_ref, r3_ref):
                values, more = decode(ref, index)
                total += values
                count += more
            if d == 0:
                out_ref[c, pl.ds(0, HALF), :] = total
                out_ref[c, pl.ds(HALF, 8), :] = jnp.broadcast_to(count, (8, BLK))
            else:
                coded, tail = encode(total, count)
                out_ref[c, pl.ds(0, HALF), :] = coded
                out_ref[c, pl.ds(HALF, 16), :] = tail


def merge_x(pos, received, own):
    coded = jax.ShapeDtypeStruct((2, HALF + 16, BLK), jnp.int16)
    return pl.pallas_call(
        merge_x_kernel,
        out_shape=(jax.ShapeDtypeStruct((2, HALF + 8, BLK), jnp.float32), coded, coded, coded),
        in_specs=[SMEM] + [VMEM] * 4,
        out_specs=[VMEM] * 4,
        compiler_params=PARAMS,
        name="merge_x",
    )(pos, *received, own)


def merge_z_kernel(pos_ref, r1_ref, r2_ref, r3_ref, own_ref, mine_ref, theirs_ref):
    core = pos_ref[2]
    for out_ref, index in ((mine_ref, core), (theirs_ref, 1 - core)):
        total = own_ref[index, pl.ds(0, HALF), :]
        count = own_ref[index, pl.ds(HALF, 8), :][0:1]
        for ref in (r1_ref, r2_ref, r3_ref):
            values, more = decode(ref, index)
            total += values
            count += more
        out_ref[...] = (total / jnp.sqrt(1.0 + count)).astype(jnp.bfloat16)


def merge_z(pos, received, own):
    half = jax.ShapeDtypeStruct((HALF, BLK), jnp.bfloat16)
    return pl.pallas_call(
        merge_z_kernel,
        out_shape=(half, half),
        in_specs=[SMEM] + [VMEM] * 4,
        out_specs=[VMEM] * 2,
        compiler_params=PARAMS,
        name="merge_z",
    )(pos, *received, own)


def pre_kernel(pos_ref, mine_ref, other_ref, w_mine_ref, w_other_ref, self_ref, own_ref, o1_ref, o2_ref, o3_ref, acc):
    y = pos_ref[3]
    contract = (((0,), (0,)), ((), ()))
    acc[...] = (
        self_ref[...]
        + lax.dot_general(mine_ref[...], w_mine_ref[...], contract, preferred_element_type=jnp.float32)
        + lax.dot_general(other_ref[...], w_other_ref[...], contract, preferred_element_type=jnp.float32)
    )
    for d, out_ref in enumerate((own_ref, o1_ref, o2_ref, o3_ref)):
        out_ref[...] = acc[pl.ds(pl.multiple_of(lax.rem(y + d, NY) * 32, 32), 32), :]


def pre_terms(pos, mine, other, w_mine, w_other, self_term):
    hid = w_mine.shape[1]
    part = jax.ShapeDtypeStruct((BLK // NY, hid), jnp.float32)
    return pl.pallas_call(
        pre_kernel,
        out_shape=(part,) * 4,
        in_specs=[SMEM] + [VMEM] * 5,
        out_specs=[VMEM] * 4,
        scratch_shapes=[pltpu.VMEM((BLK, hid), jnp.float32)],
        compiler_params=PARAMS,
        name="pre_terms",
    )(pos, mine, other, w_mine, w_other, self_term)


def gather_kernel(pos_ref, own_ref, r1_ref, r2_ref, r3_ref, out_ref):
    y = pos_ref[3]
    for d, ref in enumerate((own_ref, r1_ref, r2_ref, r3_ref)):
        out_ref[pl.ds(pl.multiple_of(lax.rem(y + NY - d, NY) * 32, 32), 32), :] = ref[...]


def gather_hidden(pos, own, received):
    hid = own.shape[1]
    return pl.pallas_call(
        gather_kernel,
        out_shape=jax.ShapeDtypeStruct((BLK, hid), jnp.bfloat16),
        in_specs=[SMEM] + [VMEM] * 4,
        out_specs=VMEM,
        compiler_params=PARAMS,
        name="gather_hidden",
    )(pos, own, *received)


def grads_kernel(
    pos_ref, hid0_ref, hid1_ref, og0_ref, og1_ref, agg0_ref, agg1_ref, seed0_ref, seed1_ref,
    own_ref, o1_ref, o2_ref, o3_ref, acc_self, acc_neigh, bias,
):
    x = pos_ref[0]
    hid = hid0_ref.shape[1]
    zero = jnp.zeros_like(og0_ref)
    rows0 = jnp.where(hid0_ref[...] > 0, og0_ref[...], zero)
    rows1 = jnp.where(hid1_ref[...] > 0, og1_ref[...], zero)
    dot = functools.partial(jnp.dot, preferred_element_type=jnp.float32)
    acc_self[...] = dot(seed0_ref[...], rows0) + dot(seed1_ref[...], rows1)
    acc_neigh[...] = dot(agg0_ref[...], rows0) + dot(agg1_ref[...], rows1)
    total = jnp.sum(rows0.astype(jnp.float32), axis=0, keepdims=True) + jnp.sum(
        rows1.astype(jnp.float32), axis=0, keepdims=True
    )
    for part in range(8):
        bias[pl.ds(part, 1), :] = total[:, part * BLK:(part + 1) * BLK]
    row = lax.broadcasted_iota(jnp.int32, (16, BLK), 0)
    for d, out_ref in enumerate((own_ref, o1_ref, o2_ref, o3_ref)):
        to = lax.rem(x + d, NX)
        rows = pl.ds(pl.multiple_of(to * 64, 64), 64)
        out_ref[pl.ds(0, 64), pl.ds(0, hid)] = acc_self[rows, :].astype(out_ref.dtype)
        out_ref[pl.ds(64, 64), pl.ds(0, hid)] = acc_neigh[rows, :].astype(out_ref.dtype)
        tail = jnp.where(row == 0, bias[pl.ds(to * 2, 1), :], jnp.where(row == 1, bias[pl.ds(to * 2 + 1, 1), :], 0.0))
        if d > 0:
            high = tail.astype(jnp.bfloat16).astype(jnp.float32)
            low = tail - high
            low = jnp.concatenate([jnp.zeros((2, BLK), jnp.float32), low[:14]], axis=0)
            tail = high + low
        out_ref[pl.ds(0, 16), pl.ds(hid, BLK)] = tail.astype(out_ref.dtype)
        out_ref[pl.ds(16, 112), pl.ds(hid, BLK)] = jnp.zeros((112, BLK), out_ref.dtype)


def grads(pos, hid0, hid1, og0, og1, agg0, agg1, seed0, seed1):
    hid = hid0.shape[1]
    part = jax.ShapeDtypeStruct((BLK, hid + BLK), jnp.bfloat16)
    own = jax.ShapeDtypeStruct((BLK, hid + BLK), jnp.float32)
    return pl.pallas_call(
        grads_kernel,
        out_shape=(own, part, part, part),
        in_specs=[SMEM] + [VMEM] * 8,
        out_specs=[VMEM] * 4,
        scratch_shapes=[
            pltpu.VMEM((HALF, hid), jnp.float32),
            pltpu.VMEM((HALF, hid), jnp.float32),
            pltpu.VMEM((8, BLK), jnp.float32),
        ],
        compiler_params=PARAMS,
        name="grads",
    )(pos, hid0, hid1, og0, og1, agg0, agg1, seed0, seed1)


def merge_gx_kernel(pos_ref, r1_ref, r2_ref, r3_ref, own_ref, kept_ref, o1_ref, o2_ref, o3_ref, total, bias):
    z = pos_ref[1]
    hid = own_ref.shape[1] - BLK
    body = own_ref[:, pl.ds(0, hid)]
    tail = own_ref[pl.ds(0, 16), pl.ds(hid, BLK)]
    for ref in (r1_ref, r2_ref, r3_ref):
        body += ref[:, pl.ds(0, hid)].astype(jnp.float32)
        tail += ref[pl.ds(0, 16), pl.ds(hid, BLK)].astype(jnp.float32)
    total[...] = body
    bias[...] = jnp.concatenate([tail[0:2] + tail[2:4], jnp.zeros((6, BLK), jnp.float32)], axis=0)
    row = lax.broadcasted_iota(jnp.int32, (16, BLK), 0)
    for d, out_ref in enumerate((kept_ref, o1_ref, o2_ref, o3_ref)):
        to = lax.rem(z + d, NZ)
        out_ref[pl.ds(0, 16), pl.ds(0, hid)] = total[pl.ds(pl.multiple_of(to * 16, 16), 16), :].astype(out_ref.dtype)
        out_ref[pl.ds(16, 16), pl.ds(0, hid)] = total[pl.ds(pl.multiple_of(64 + to * 16, 16), 16), :].astype(out_ref.dtype)
        line = bias[pl.ds(to // 2, 1), :]
        if d > 0:
            high = line.astype(jnp.bfloat16).astype(jnp.float32)
            mark = jnp.where(row == 0, high, jnp.where(row == 1, line - high, 0.0))
        else:
            mark = jnp.where(row == 0, line, 0.0)
        out_ref[pl.ds(0, 16), pl.ds(hid, BLK)] = mark.astype(out_ref.dtype)
        out_ref[pl.ds(16, 16), pl.ds(hid, BLK)] = jnp.zeros((16, BLK), out_ref.dtype)


def merge_gx(pos, received, own):
    width = own.shape[1]
    part = jax.ShapeDtypeStruct((32, width), jnp.bfloat16)
    return pl.pallas_call(
        merge_gx_kernel,
        out_shape=(jax.ShapeDtypeStruct((32, width), jnp.float32), part, part, part),
        in_specs=[SMEM] + [VMEM] * 4,
        out_specs=[VMEM] * 4,
        scratch_shapes=[pltpu.VMEM((BLK, width - BLK), jnp.float32), pltpu.VMEM((8, BLK), jnp.float32)],
        compiler_params=PARAMS,
        name="merge_gx",
    )(pos, *received, own)


def merge_gz_kernel(r1_ref, r2_ref, r3_ref, own_ref, self_ref, neigh_ref, bias_ref):
    hid = self_ref.shape[1]
    body = own_ref[:, pl.ds(0, hid)]
    tail = own_ref[pl.ds(0, 16), pl.ds(hid, BLK)]
    for ref in (r1_ref, r2_ref, r3_ref):
        body += ref[:, pl.ds(0, hid)].astype(jnp.float32)
        tail += ref[pl.ds(0, 16), pl.ds(hid, BLK)].astype(jnp.float32)
    self_ref[...] = body[:16]
    neigh_ref[...] = body[16:]
    bias_ref[...] = jnp.broadcast_to(tail[0:1] + tail[1:2], (8, BLK))


def merge_gz(received, own):
    hid = own.shape[1] - BLK
    part = jax.ShapeDtypeStruct((16, hid), jnp.float32)
    return pl.pallas_call(
        merge_gz_kernel,
        out_shape=(part, part, jax.ShapeDtypeStruct((8, BLK), jnp.float32)),
        in_specs=[VMEM] * 4,
        out_specs=[VMEM] * 3,
        compiler_params=PARAMS,
        name="merge_gz",
    )(*received, own)


def halves(weights, core):
    hid = weights.shape[1]
    cut = weights.reshape(16, 2, 16, hid)
    take = lambda c: lax.dynamic_index_in_dim(cut, c, 1, keepdims=False).reshape(HALF, hid)
    return take(core), take(1 - core)


def body(features, seed_feats, patterns, sources, counts, w_self, w_neigh, bias_term, out_grad):
    node = lax.axis_index("node")
    feat = lax.axis_index("feat")
    x, z, core = node // (NZ * 2), (node // 2) % NZ, node % 2
    y = feat % NY
    pos = jnp.stack([x, z, core, y]).astype(jnp.int32)
    swap = lambda value: lax.ppermute(value, "node", SWAP_CORE)

    packed = patterns.transpose(0, 1, 3, 2)
    table = jnp.concatenate([counts, sources.reshape(-1)])
    packed_other, table_other = swap(packed), swap(table)
    mine, theirs, seed_mine, seed_theirs = split(pos[2:3], features, seed_feats)
    other, seed_other = swap(theirs), swap(seed_theirs)
    out_grad_other = swap(out_grad)
    lists = counts.shape[0]
    table = jnp.concatenate([table[:lists], table_other[:lists], table[lists:], table_other[lists:]])

    received = []
    for d in (2, 1, 3):
        meta = jnp.concatenate([((x + d) % NX * 8)[None].astype(jnp.int32), table])
        coded = sums(True, meta, packed, packed_other, mine, other)
        received.append(lax.ppermute(coded, "node", shift_x(d)))
    meta = jnp.concatenate([(x * 8)[None].astype(jnp.int32), table])
    own = sums(False, meta, packed, packed_other, mine, other)
    self_term = jnp.dot(seed_feats, w_self, preferred_element_type=jnp.float32)
    w_mine, w_other = halves(w_neigh, core)

    own, *coded = merge_x(pos, received, own)
    received = [lax.ppermute(coded[d - 1], "node", shift_z(d)) for d in (2, 1, 3)]
    agg_mine, agg_theirs = merge_z(pos, received, own)
    agg_other = swap(agg_theirs)

    own, *parts = pre_terms(pos, agg_mine, agg_other, w_mine, w_other, self_term)
    received = [lax.ppermute(parts[d - 1], "feat", shift_y(d)) for d in (2, 1, 3)]
    part = own + received[0] + received[1] + received[2]
    pre = part + lax.ppermute(part, "feat", SWAP_FAR) + bias_term
    own = jnp.maximum(pre, 0.0).astype(jnp.bfloat16)
    received = [lax.ppermute(own, "feat", shift_y(d)) for d in (1, 2, 3)]
    hidden = gather_hidden(pos, own, received)
    hidden_other = swap(hidden)

    own, *parts = grads(
        pos, hidden, hidden_other, out_grad, out_grad_other, agg_mine, agg_theirs, seed_mine, seed_other
    )
    received = [lax.ppermute(parts[d - 1], "node", shift_x(d)) for d in (2, 1, 3)]
    own, *parts = merge_gx(pos, received, own)
    received = [lax.ppermute(parts[d - 1], "node", shift_z(d)) for d in (2, 1, 3)]
    grad_self, grad_neigh, bias = merge_gz(received, own)
    grad_bias = lax.dynamic_slice(bias[0], (z % 2 * 64 + core * 32,), (32,))
    return (hidden, grad_self, grad_neigh, grad_bias)


def solution(mesh):
    return jax.shard_map(
        body,
        mesh=mesh,
        in_specs=(
            P("node", "feat"),
            P("node", "feat"),
            P("node", None, None, None),
            P("node", None),
            P("node"),
            P("feat", None),
            P("feat", None),
            P(),
            P("node", None),
        ),
        out_specs=(
            P("node", None),
            P(("feat", "node"), None),
            P(("feat", "node"), None),
            P("node"),
        ),
        check_vma=False,
    )
```

time: 659 us -> 141 us (0.21)
  the two profiles are of different devices: /device:TPU:16 before, /device:TPU:6 now
where the time goes in v1:
time: 141 us; the launch traced here: 139 us
  waiting for transfers between devices  47.6 us (34%)
  Pallas kernels  43 us (30%)
  starting transfers between devices  37.1 us (26%)
  local copies, waits for them, and re-layouts  9.38 us (7%)
    pallas_call x4, Pallas kernels, sums(): pl.pallas_call(functools.partial(sums_kernel, coded_out), out_shape=jax.S...  33.7 us
    ppermute x3, waiting for transfers between devices, body(): lax.ppermute(parts[d - 1], 'node', shift_x(d))  14.5 us
    ppermute x3, starting transfers between devices, body(): lax.ppermute(parts[d - 1], 'node', shift_z(d))  8.77 us
    unnamed x33, local copies, waits for them, and re-layouts  8.21 us
    ppermute x3, starting transfers between devices, body(): lax.ppermute(coded[d - 1], 'node', shift_z(d))  8.16 us
    ppermute x3, waiting for transfers between devices, body(): lax.ppermute(parts[d - 1], 'feat', shift_y(d))  7.09 us
    ppermute x3, waiting for transfers between devices, body(): lax.ppermute(coded[d - 1], 'node', shift_z(d))  6.5 us
    ppermute x3, starting transfers between devices, body(): lax.ppermute(parts[d - 1], 'feat', shift_y(d))  5.49 us
  transfers between devices with their start and end apart: 26, of which 16 were waited for; matrix products, arithmetic and copies ran while one was open for 1% of the time, Pallas kernels for 22%

profile of v1, /device:TPU:6, one launch (start us, length us, event | category | flops | bytes accessed | tf_op | source)
XLA Modules:
  0.0 138.5 jit_solution(15534998736417991360)
XLA Ops:
  0.7 0.1 collective-permute-start.1
  0.8 1.6 %copy-done.1 = bf16[2048,512]{1,0:T(8,128)(2,1)S(1)} copy-done((bf16[2048,512]{1,0:T(8,128)(2,1)S(1)}, bf16[2048,512]{1,0:T(8,128)(2,1)}, u32[]{:S(2)}) %copy-start.1) | copy-done | bytes 2097176
  2.4 0.9 copy-done.3
  3.3 2.5 %split.1 = (bf16[256,2048]{1,0:T(8,128)(2,1)S(1)}, bf16[256,2048]{1,0:T(8,128)(2,1)}, bf16[256,128]{1,0:T(8,128)(2,1)S(1)}, bf16[256,128]{1,0:T(8,128)(2,1)S(1)}) custom-call(s32[1]{0:T(128)} %bitcast.2.core_ref, bf16[2048,512]{1,0:T(8,128)(2,1)S(1)} %copy-done.1, bf16[128,512]{1,0:T(8,128)(2,1)S(1)} %copy-done.3), custom_call_target="tpu_custom_call" | custom-call | tf_op jit(solution)/shard_map/split/pallas_call | solution.py:74
  5.7 1.0 copy-done.9
  6.7 0.5 collective-permute-start.2
  7.3 0.1 reshape.24
  7.5 1.9 %collective-permute-done = s32[288]{0:T(512)S(1)} collective-permute-done((s32[288]{0:T(512)S(1)}, s32[288]{0:T(512)S(1)}, u32[]{:S(2)}, u32[]{:S(2)}) %collective-permute-start) | collective-permute-done | bytes 1184 | tf_op jit(solution)/shard_map/ppermute | solution.py:396
  9.6 0.1 concatenate.21.meta_ref
  9.6 0.1 concatenate.22.meta_ref
  9.7 0.1 concatenate.23.meta_ref
  9.8 1.2 copy-done.10
  11.1 7.6 %sums.4 = s16[8,272,128]{2,1,0:T(8,128)(2,1)S(1)} custom-call(s32[577]{0:T(1024)S(1)} %concatenate.21.meta_ref, s32[32,8,8,128]{3,2,1,0:T(8,128)S(1)} %bitcast.23, s32[32,8,8,128]{3,2,1,0:T(8,128)} %collective-permute-done.1.pat1_ref, bf16[256,2048]{1,0:T(8,128)(2,1)S(1)} %copy-done.10, bf16[256,2048]{1,0:T(8,128)(2,1)} %collective-permute-done.2.feat1_ref), custom_call_target="tpu_custom_call" | custom-call | flops 2000000000 | bytes 3000000 | tf_op jit(solution)/shard_map/sums/pallas_call | solution.py:151
  18.6 1.0 collective-permute-start.3
  19.6 9.3 %sums.5 = s16[8,272,128]{2,1,0:T(8,128)(2,1)} custom-call(s32[577]{0:T(1024)S(1)} %concatenate.22.meta_ref, s32[32,8,8,128]{3,2,1,0:T(8,128)S(1)} %bitcast.24, s32[32,8,8,128]{3,2,1,0:T(8,128)} %collective-permute-done.1.pat1_ref, bf16[256,2048]{1,0:T(8,128)(2,1)S(1)} %copy-done.10, bf16[256,2048]{1,0:T(8,128)(2,1)} %collective-permute-done.2.feat1_ref), custom_call_target="tpu_custom_call" | custom-call | flops 2000000000 | bytes 3000000 | tf_op jit(solution)/shard_map/sums/pallas_call | solution.py:151
  29.0 1.3 collective-permute-start.4
  30.2 8.6 %sums.6 = s16[8,272,128]{2,1,0:T(8,128)(2,1)} custom-call(s32[577]{0:T(1024)S(1)} %concatenate.23.meta_ref, s32[32,8,8,128]{3,2,1,0:T(8,128)S(1)} %bitcast.25, s32[32,8,8,128]{3,2,1,0:T(8,128)} %collective-permute-done.1.pat1_ref, bf16[256,2048]{1,0:T(8,128)(2,1)S(1)} %copy-done.10, bf16[256,2048]{1,0:T(8,128)(2,1)} %collective-permute-done.2.feat1_ref), custom_call_target="tpu_custom_call" | custom-call | flops 2000000000 | bytes 3000000 | tf_op jit(solution)/shard_map/sums/pallas_call | solution.py:151
  38.9 0.2 collective-permute-start.5
  39.1 0.1 concatenate.24.meta_ref
  39.2 1.2 copy-done.8
  40.4 1.2 copy-done.11
  41.6 8.1 %sums.7.own_ref = f32[8,264,128]{2,1,0:T(8,128)S(1)} custom-call(s32[577]{0:T(1024)S(1)} %concatenate.24.meta_ref, s32[32,8,8,128]{3,2,1,0:T(8,128)S(1)} %bitcast.26, s32[32,8,8,128]{3,2,1,0:T(8,128)} %collective-permute-done.1.pat1_ref, bf16[256,2048]{1,0:T(8,128)(2,1)S(1)} %copy-done.11, bf16[256,2048]{1,0:T(8,128)(2,1)} %collective-permute-done.2.feat1_ref), custom_call_target="tpu_custom_call" | custom-call | flops 2000000000 | bytes 3000000 | tf_op jit(solution)/shard_map/sums/pallas_call | solution.py:151
  49.8 4.8 %collective-permute-done.5.r3_ref = s16[8,272,128]{2,1,0:T(8,128)(2,1)S(1)} collective-permute-done((s16[8,272,128]{2,1,0:T(8,128)(2,1)}, s16[8,272,128]{2,1,0:T(8,128)(2,1)S(1)}, u32[]{:S(2)}, u32[]{:S(2)}) %collective-permute-start.5) | collective-permute-done | bytes 557088 | tf_op jit(solution)/shard_map/ppermute | solution.py:411
  54.6 1.1 merge_x.1
  55.7 4.3 %collective-permute-start.6 = (s16[2,272,128]{2,1,0:T(8,128)(2,1)S(1)}, s16[2,272,128]{2,1,0:T(8,128)(2,1)S(1)}, u32[]{:S(2)}, u32[]{:S(2)}) collective-permute-start(s16[2,272,128]{2,1,0:T(8,128)(2,1)S(1)} %get-tuple-element.31), channel_id=1, source_target_pairs={{0,4},{1,5},{2,6},{3,7},{4,0},{5,1},{6,2},{7,3},{8,12},{9,13},{10,... | collective-permute-start | bytes 417800 | tf_op jit(solution)/shard_map/ppermute | solution.py:418
  60.1 1.7 %collective-permute-start.7 = (s16[2,272,128]{2,1,0:T(8,128)(2,1)S(1)}, s16[2,272,128]{2,1,0:T(8,128)(2,1)S(1)}, u32[]{:S(2)}, u32[]{:S(2)}) collective-permute-start(s16[2,272,128]{2,1,0:T(8,128)(2,1)S(1)} %get-tuple-element.32), channel_id=1, source_target_pairs={{0,2},{1,3},{2,4},{3,5},{4,6},{5,7},{6,0},{7,1},{8,10},{9,11},{10,... | collective-permute-start | bytes 417800 | tf_op jit(solution)/shard_map/ppermute | solution.py:418
  61.8 2.1 %collective-permute-start.8 = (s16[2,272,128]{2,1,0:T(8,128)(2,1)S(1)}, s16[2,272,128]{2,1,0:T(8,128)(2,1)S(1)}, u32[]{:S(2)}, u32[]{:S(2)}) collective-permute-start(s16[2,272,128]{2,1,0:T(8,128)(2,1)S(1)} %get-tuple-element.33), channel_id=1, source_target_pairs={{0,6},{1,7},{2,0},{3,1},{4,2},{5,3},{6,4},{7,5},{8,14},{9,15},{10,... | collective-permute-start | bytes 417800 | tf_op jit(solution)/shard_map/ppermute | solution.py:418
  63.9 0.3 fusion.1.self_ref
  64.2 6.2 %collective-permute-done.6.r1_ref = s16[2,272,128]{2,1,0:T(8,128)(2,1)S(1)} collective-permute-done((s16[2,272,128]{2,1,0:T(8,128)(2,1)S(1)}, s16[2,272,128]{2,1,0:T(8,128)(2,1)S(1)}, u32[]{:S(2)}, u32[]{:S(2)}) %collective-permute-start.6) | collective-permute-done | bytes 139296 | tf_op jit(solution)/shard_map/ppermute | solution.py:418
  70.5 0.2 collective-permute-done.8.r3_ref
  70.7 0.7 merge_z.1
  71.4 0.1 collective-permute-start.9
  71.5 0.1 constant_dynamic-slice_fusion.1
  71.7 1.1 collective-permute-done.9.other_ref
  72.8 0.9 pre_terms.1
  73.7 3.3 %collective-permute-start.12 = (f32[32,1024]{1,0:T(8,128)S(1)}, f32[32,1024]{1,0:T(8,128)S(1)}, u32[]{:S(2)}, u32[]{:S(2)}) collective-permute-start(f32[32,1024]{1,0:T(8,128)S(1)} %get-tuple-element.40), channel_id=1, source_target_pairs={{0,96},{32,0},{64,32},{96,64},{128,224},{160,128},{192,160},{224,1... | collective-permute-start | bytes 393224 | tf_op jit(solution)/shard_map/ppermute | solution.py:423
  77.0 2.2 %collective-permute-start.10 = (f32[32,1024]{1,0:T(8,128)S(1)}, f32[32,1024]{1,0:T(8,128)S(1)}, u32[]{:S(2)}, u32[]{:S(2)}) collective-permute-start(f32[32,1024]{1,0:T(8,128)S(1)} %get-tuple-element.38), channel_id=1, source_target_pairs={{0,64},{32,96},{64,0},{96,32},{128,192},{160,224},{192,128},{224,1... | collective-permute-start | bytes 393224 | tf_op jit(solution)/shard_map/ppermute | solution.py:423
  79.2 0.9 collective-permute-done.12
  80.0 6.2 %collective-permute-done.11 = f32[32,1024]{1,0:T(8,128)S(1)} collective-permute-done((f32[32,1024]{1,0:T(8,128)S(1)}, f32[32,1024]{1,0:T(8,128)S(1)}, u32[]{:S(2)}, u32[]{:S(2)}) %collective-permute-start.11) | collective-permute-done | bytes 131104 | tf_op jit(solution)/shard_map/ppermute | solution.py:423
  86.3 5.2 %collective-permute-start.13 = (f32[32,1024]{1,0:T(8,128)S(1)}, f32[32,1024]{1,0:T(8,128)S(1)}, u32[]{:S(2)}, u32[]{:S(2)}) collective-permute-start(f32[32,1024]{1,0:T(8,128)S(1)} %add_add_fusion), channel_id=1, source_target_pairs={{0,128},{32,160},{64,192},{96,224},{128,0},{160,32},{192,64},{224,... | collective-permute-start | bytes 393224 | tf_op jit(solution)/shard_map/ppermute | solution.py:425
  91.5 3.7 %collective-permute-done.13 = f32[32,1024]{1,0:T(8,128)S(1)} collective-permute-done((f32[32,1024]{1,0:T(8,128)S(1)}, f32[32,1024]{1,0:T(8,128)S(1)}, u32[]{:S(2)}, u32[]{:S(2)}) %collective-permute-start.13) | collective-permute-done | bytes 131104 | tf_op jit(solution)/shard_map/ppermute | solution.py:425
  95.3 0.1 collective-permute-start.14
  95.4 2.0 %collective-permute-start.15 = (bf16[32,1024]{1,0:T(8,128)(2,1)S(1)}, bf16[32,1024]{1,0:T(8,128)(2,1)S(1)}, u32[]{:S(2)}, u32[]{:S(2)}) collective-permute-start(bf16[32,1024]{1,0:T(8,128)(2,1)S(1)} %maximum_convert_fusion.own_ref), channel_id=1, source_target_pairs={{0,64},{32,96},{64,0},{96,32},{128,192},{160,224},{192,128},{224,1... | collective-permute-start | bytes 196616 | tf_op jit(solution)/shard_map/ppermute | solution.py:427
  97.4 1.2 collective-permute-start.16
  98.6 2.9 %collective-permute-done.14.r1_ref = bf16[32,1024]{1,0:T(8,128)(2,1)S(1)} collective-permute-done((bf16[32,1024]{1,0:T(8,128)(2,1)S(1)}, bf16[32,1024]{1,0:T(8,128)(2,1)S(1)}, u32[]{:S(2)}, u32[]{:S(2)}) %collective-permute-start.14) | collective-permute-done | bytes 65568 | tf_op jit(solution)/shard_map/ppermute | solution.py:427
  101.6 0.9 collective-permute-done.16.r3_ref
  102.4 1.3 gather_hidden.1.hid0_ref
  103.7 0.5 collective-permute-start.19
  104.2 0.9 collective-permute-done.19.seed1_ref
  105.1 0.4 collective-permute-done.17.hid1_ref
  105.5 0.9 copy-done.2
  106.5 1.5 %grads.1 = (f32[128,1152]{1,0:T(8,128)S(1)}, bf16[128,1152]{1,0:T(8,128)(2,1)S(1)}, bf16[128,1152]{1,0:T(8,128)(2,1)S(1)}, bf16[128,1152]{1,0:T(8,128)(2,1)S(1)}) custom-call(s32[4]{0:T(128)S(1)} %pad_add_fusion.1.pos_ref, bf16[128,1024]{1,0:T(8,128)(2,1)S(1)} %copy-done.2, bf16[128,1024]{1,0:T(8,128)(2,1)S(1)} %collective-permute-done.17.hid1_ref, ...), custom_call_target="tpu_custom_call" | custom-call | tf_op jit(solution)/shard_map/grads/pallas_call | solution.py:304
  108.0 0.5 collective-permute-start.20
  108.4 1.9 %collective-permute-start.21 = (bf16[128,1152]{1,0:T(8,128)(2,1)S(1)}, bf16[128,1152]{1,0:T(8,128)(2,1)S(1)}, u32[]{:S(2)}, u32[]{:S(2)}) collective-permute-start(bf16[128,1152]{1,0:T(8,128)(2,1)S(1)} %get-tuple-element.44), channel_id=1, source_target_pairs={{0,8},{1,9},{2,10},{3,11},{4,12},{5,13},{6,14},{7,15},{8,16},{9,17... | collective-permute-start | bytes 884744 | tf_op jit(solution)/shard_map/ppermute | solution.py:434
  110.3 0.1 collective-permute-start.22
  110.5 9.0 %collective-permute-done.20.r1_ref = bf16[128,1152]{1,0:T(8,128)(2,1)S(1)} collective-permute-done((bf16[128,1152]{1,0:T(8,128)(2,1)S(1)}, bf16[128,1152]{1,0:T(8,128)(2,1)S(1)}, u32[]{:S(2)}, u32[]{:S(2)}) %collective-permute-start.20) | collective-permute-done | bytes 294944 | tf_op jit(solution)/shard_map/ppermute | solution.py:434
  119.5 2.5 %collective-permute-done.21.r2_ref = bf16[128,1152]{1,0:T(8,128)(2,1)S(1)} collective-permute-done((bf16[128,1152]{1,0:T(8,128)(2,1)S(1)}, bf16[128,1152]{1,0:T(8,128)(2,1)S(1)}, u32[]{:S(2)}, u32[]{:S(2)}) %collective-permute-start.21) | collective-permute-done | bytes 294944 | tf_op jit(solution)/shard_map/ppermute | solution.py:434
  121.9 3.0 %collective-permute-done.22.r3_ref = bf16[128,1152]{1,0:T(8,128)(2,1)S(1)} collective-permute-done((bf16[128,1152]{1,0:T(8,128)(2,1)S(1)}, bf16[128,1152]{1,0:T(8,128)(2,1)S(1)}, u32[]{:S(2)}, u32[]{:S(2)}) %collective-permute-start.22) | collective-permute-done | bytes 294944 | tf_op jit(solution)/shard_map/ppermute | solution.py:434
  124.9 0.8 merge_gx.1
  125.7 5.0 %collective-permute-start.23 = (bf16[32,1152]{1,0:T(8,128)(2,1)S(1)}, bf16[32,1152]{1,0:T(8,128)(2,1)S(1)}, u32[]{:S(2)}, u32[]{:S(2)}) collective-permute-start(bf16[32,1152]{1,0:T(8,128)(2,1)S(1)} %get-tuple-element.47), channel_id=1, source_target_pairs={{0,4},{1,5},{2,6},{3,7},{4,0},{5,1},{6,2},{7,3},{8,12},{9,13},{10,... | collective-permute-start | bytes 221192 | tf_op jit(solution)/shard_map/ppermute | solution.py:436
  130.6 3.8 %collective-permute-start.25 = (bf16[32,1152]{1,0:T(8,128)(2,1)S(1)}, bf16[32,1152]{1,0:T(8,128)(2,1)S(1)}, u32[]{:S(2)}, u32[]{:S(2)}) collective-permute-start(bf16[32,1152]{1,0:T(8,128)(2,1)S(1)} %get-tuple-element.49), channel_id=1, source_target_pairs={{0,6},{1,7},{2,0},{3,1},{4,2},{5,3},{6,4},{7,5},{8,14},{9,15},{10,... | collective-permute-start | bytes 221192 | tf_op jit(solution)/shard_map/ppermute | solution.py:436
  134.5 2.8 %collective-permute-done.24.r2_ref = bf16[32,1152]{1,0:T(8,128)(2,1)S(1)} collective-permute-done((bf16[32,1152]{1,0:T(8,128)(2,1)S(1)}, bf16[32,1152]{1,0:T(8,128)(2,1)S(1)}, u32[]{:S(2)}, u32[]{:S(2)}) %collective-permute-start.24) | collective-permute-done | bytes 73760 | tf_op jit(solution)/shard_map/ppermute | solution.py:436
  137.3 0.7 merge_gz.1
  138.0 0.6 fusion
  (48 shorter events, 0.5 us)
Async XLA Ops:
  0.6 63.3 %copy-start = (bf16[512,1024]{1,0:T(8,128)(2,1)S(1)}, bf16[512,1024]{1,0:T(8,128)(2,1)}, u32[]{:S(2)}) copy-start(bf16[512,1024]{1,0:T(8,128)(2,1)} %param.14) | copy-start | bytes 3145732
  0.6 6.5 %copy-start.14 = (s32[32,8]{0,1:T(8,128)S(1)}, s32[32,8]{0,1:T(8,128)}, u32[]{:S(2)}) copy-start(s32[32,8]{0,1:T(8,128)} %param.12) | copy-start | bytes 3076
  0.7 6.7 %copy-start.13 = (s32[32]{0:T(128)S(1)}, s32[32]{0:T(128)}, u32[]{:S(2)}) copy-start(s32[32]{0:T(128)} %param.13) | copy-start | bytes 388
  0.7 9.1 %collective-permute-start.1 = (s32[32,8,8,128]{3,2,1,0:T(8,128)}, s32[32,8,8,128]{3,2,1,0:T(8,128)}, u32[]{:S(2)}, u32[]{:S(2)}) collective-permute-start(s32[32,8,8,128]{3,2,1,0:T(8,128)} %bitcast.22), channel_id=1, source_target_pairs={{0,1},{1,0},{2,3},{3,2},{4,5},{5,4},{6,7},{7,6},{8,9},{9,8},{10,11... | collective-permute-start | bytes 3145736 | tf_op jit(solution)/shard_map/ppermute | solution.py:396
  0.8 1.6 %copy-start.1 = (bf16[2048,512]{1,0:T(8,128)(2,1)S(1)}, bf16[2048,512]{1,0:T(8,128)(2,1)}, u32[]{:S(2)}) copy-start(bf16[2048,512]{1,0:T(8,128)(2,1)} %feat_ref.1) | copy-start | bytes 6291460
  2.4 0.9 copy-start.3
  3.3 6.5 %copy-start.6 = (s32[32,8,128,8]{2,3,1,0:T(8,128)S(1)}, s32[32,8,128,8]{2,3,1,0:T(8,128)}, u32[]{:S(2)}) copy-start(s32[32,8,128,8]{2,3,1,0:T(8,128)} %param.11) | copy-start | bytes 3145732
  5.7 1.0 copy-start.9
  6.7 3.1 %collective-permute-start.2 = (bf16[256,2048]{1,0:T(8,128)(2,1)}, bf16[256,2048]{1,0:T(8,128)(2,1)}, u32[]{:S(2)}, u32[]{:S(2)}) collective-permute-start(bf16[256,2048]{1,0:T(8,128)(2,1)} %get-tuple-element.30), channel_id=1, source_target_pairs={{0,1},{1,0},{2,3},{3,2},{4,5},{5,4},{6,7},{7,6},{8,9},{9,8},{10,11... | collective-permute-start | bytes 3145736 | tf_op jit(solution)/shard_map/ppermute | solution.py:396
  7.4 2.0 %collective-permute-start = (s32[288]{0:T(512)S(1)}, s32[288]{0:T(512)S(1)}, u32[]{:S(2)}, u32[]{:S(2)}) collective-permute-start(s32[288]{0:T(512)S(1)} %pad_add_fusion), channel_id=1, source_target_pairs={{0,1},{1,0},{2,3},{3,2},{4,5},{5,4},{6,7},{7,6},{8,9},{9,8},{10,11... | collective-permute-start | bytes 3464 | tf_op jit(solution)/shard_map/ppermute | solution.py:396
  9.8 1.2 copy-start.10
  11.1 8.6 %copy-start.7 = (s32[32,8,128,8]{2,3,1,0:T(8,128)S(1)}, s32[32,8,128,8]{2,3,1,0:T(8,128)}, u32[]{:S(2)}) copy-start(s32[32,8,128,8]{2,3,1,0:T(8,128)} %param.11) | copy-start | bytes 3145732
  18.6 31.2 %collective-permute-start.3 = (s16[8,272,128]{2,1,0:T(8,128)(2,1)S(1)}, s16[8,272,128]{2,1,0:T(8,128)(2,1)S(1)}, u32[]{:S(2)}, u32[]{:S(2)}) collective-permute-start(s16[8,272,128]{2,1,0:T(8,128)(2,1)S(1)} %sums.4), channel_id=1, source_target_pairs={{0,16},{1,17},{2,18},{3,19},{4,20},{5,21},{6,22},{7,23},{8,24},{9,... | collective-permute-start | bytes 1671176 | tf_op jit(solution)/shard_map/ppermute | solution.py:411
  29.0 20.9 %collective-permute-start.4 = (s16[8,272,128]{2,1,0:T(8,128)(2,1)}, s16[8,272,128]{2,1,0:T(8,128)(2,1)S(1)}, u32[]{:S(2)}, u32[]{:S(2)}) collective-permute-start(s16[8,272,128]{2,1,0:T(8,128)(2,1)} %sums.5), channel_id=1, source_target_pairs={{0,8},{1,9},{2,10},{3,11},{4,12},{5,13},{6,14},{7,15},{8,16},{9,17... | collective-permute-start | bytes 1671176 | tf_op jit(solution)/shard_map/ppermute | solution.py:411
  38.9 15.7 %collective-permute-start.5 = (s16[8,272,128]{2,1,0:T(8,128)(2,1)}, s16[8,272,128]{2,1,0:T(8,128)(2,1)S(1)}, u32[]{:S(2)}, u32[]{:S(2)}) collective-permute-start(s16[8,272,128]{2,1,0:T(8,128)(2,1)} %sums.6), channel_id=1, source_target_pairs={{0,24},{1,25},{2,26},{3,27},{4,28},{5,29},{6,30},{7,31},{8,0},{9,1... | collective-permute-start | bytes 1671176 | tf_op jit(solution)/shard_map/ppermute | solution.py:411
  39.2 1.2 copy-start.8
  40.4 1.2 copy-start.11
  49.8 14.1 %copy-start.4 = (bf16[128,512]{1,0:T(8,128)(2,1)S(1)}, bf16[128,512]{1,0:T(8,128)(2,1)}, u32[]{:S(2)}) copy-start(bf16[128,512]{1,0:T(8,128)(2,1)} %seed_ref.1) | copy-start | bytes 393220
  49.8 21.7 %copy-start.12 = (bf16[512,1024]{1,0:T(8,128)(2,1)S(1)}, bf16[512,1024]{1,0:T(8,128)(2,1)}, u32[]{:S(2)}) copy-start(bf16[512,1024]{1,0:T(8,128)(2,1)} %param.15) | copy-start | bytes 3145732
  55.7 14.7 %collective-permute-start.6 = (s16[2,272,128]{2,1,0:T(8,128)(2,1)S(1)}, s16[2,272,128]{2,1,0:T(8,128)(2,1)S(1)}, u32[]{:S(2)}, u32[]{:S(2)}) collective-permute-start(s16[2,272,128]{2,1,0:T(8,128)(2,1)S(1)} %get-tuple-element.31), channel_id=1, source_target_pairs={{0,4},{1,5},{2,6},{3,7},{4,0},{5,1},{6,2},{7,3},{8,12},{9,13},{10,... | collective-permute-start | bytes 417800 | tf_op jit(solution)/shard_map/ppermute | solution.py:418
  60.1 10.4 %collective-permute-start.7 = (s16[2,272,128]{2,1,0:T(8,128)(2,1)S(1)}, s16[2,272,128]{2,1,0:T(8,128)(2,1)S(1)}, u32[]{:S(2)}, u32[]{:S(2)}) collective-permute-start(s16[2,272,128]{2,1,0:T(8,128)(2,1)S(1)} %get-tuple-element.32), channel_id=1, source_target_pairs={{0,2},{1,3},{2,4},{3,5},{4,6},{5,7},{6,0},{7,1},{8,10},{9,11},{10,... | collective-permute-start | bytes 417800 | tf_op jit(solution)/shard_map/ppermute | solution.py:418
  61.8 9.0 %collective-permute-start.8 = (s16[2,272,128]{2,1,0:T(8,128)(2,1)S(1)}, s16[2,272,128]{2,1,0:T(8,128)(2,1)S(1)}, u32[]{:S(2)}, u32[]{:S(2)}) collective-permute-start(s16[2,272,128]{2,1,0:T(8,128)(2,1)S(1)} %get-tuple-element.33), channel_id=1, source_target_pairs={{0,6},{1,7},{2,0},{3,1},{4,2},{5,3},{6,4},{7,5},{8,14},{9,15},{10,... | collective-permute-start | bytes 417800 | tf_op jit(solution)/shard_map/ppermute | solution.py:418
  71.4 1.3 collective-permute-start.9
  71.5 23.7 %copy-start.15 = (f32[1024]{0:T(1024)S(1)}, f32[1024]{0:T(1024)}, u32[]{:S(2)}) copy-start(f32[1024]{0:T(1024)} %param.16) | copy-start | bytes 12292
  71.5 27.1 %copy-start.5 = (bf16[128,1024]{1,0:T(8,128)(2,1)S(1)}, bf16[128,1024]{1,0:T(8,128)(2,1)}, u32[]{:S(2)}) copy-start(bf16[128,1024]{1,0:T(8,128)(2,1)} %og0_ref.1) | copy-start | bytes 786436
  73.7 6.4 %collective-permute-start.12 = (f32[32,1024]{1,0:T(8,128)S(1)}, f32[32,1024]{1,0:T(8,128)S(1)}, u32[]{:S(2)}, u32[]{:S(2)}) collective-permute-start(f32[32,1024]{1,0:T(8,128)S(1)} %get-tuple-element.40), channel_id=1, source_target_pairs={{0,96},{32,0},{64,32},{96,64},{128,224},{160,128},{192,160},{224,1... | collective-permute-start | bytes 393224 | tf_op jit(solution)/shard_map/ppermute | solution.py:423
  77.0 9.3 %collective-permute-start.11 = (f32[32,1024]{1,0:T(8,128)S(1)}, f32[32,1024]{1,0:T(8,128)S(1)}, u32[]{:S(2)}, u32[]{:S(2)}) collective-permute-start(f32[32,1024]{1,0:T(8,128)S(1)} %get-tuple-element.39), channel_id=1, source_target_pairs={{0,32},{32,64},{64,96},{96,0},{128,160},{160,192},{192,224},{224,1... | collective-permute-start | bytes 393224 | tf_op jit(solution)/shard_map/ppermute | solution.py:423
  77.0 9.3 %collective-permute-start.10 = (f32[32,1024]{1,0:T(8,128)S(1)}, f32[32,1024]{1,0:T(8,128)S(1)}, u32[]{:S(2)}, u32[]{:S(2)}) collective-permute-start(f32[32,1024]{1,0:T(8,128)S(1)} %get-tuple-element.38), channel_id=1, source_target_pairs={{0,64},{32,96},{64,0},{96,32},{128,192},{160,224},{192,128},{224,1... | collective-permute-start | bytes 393224 | tf_op jit(solution)/shard_map/ppermute | solution.py:423
  86.3 9.0 %collective-permute-start.13 = (f32[32,1024]{1,0:T(8,128)S(1)}, f32[32,1024]{1,0:T(8,128)S(1)}, u32[]{:S(2)}, u32[]{:S(2)}) collective-permute-start(f32[32,1024]{1,0:T(8,128)S(1)} %add_add_fusion), channel_id=1, source_target_pairs={{0,128},{32,160},{64,192},{96,224},{128,0},{160,32},{192,64},{224,... | collective-permute-start | bytes 393224 | tf_op jit(solution)/shard_map/ppermute | solution.py:425
  95.3 6.3 %collective-permute-start.14 = (bf16[32,1024]{1,0:T(8,128)(2,1)S(1)}, bf16[32,1024]{1,0:T(8,128)(2,1)S(1)}, u32[]{:S(2)}, u32[]{:S(2)}) collective-permute-start(bf16[32,1024]{1,0:T(8,128)(2,1)S(1)} %maximum_convert_fusion.own_ref), channel_id=1, source_target_pairs={{0,32},{32,64},{64,96},{96,0},{128,160},{160,192},{192,224},{224,1... | collective-permute-start | bytes 196616 | tf_op jit(solution)/shard_map/ppermute | solution.py:427
  95.4 6.2 %collective-permute-start.15 = (bf16[32,1024]{1,0:T(8,128)(2,1)S(1)}, bf16[32,1024]{1,0:T(8,128)(2,1)S(1)}, u32[]{:S(2)}, u32[]{:S(2)}) collective-permute-start(bf16[32,1024]{1,0:T(8,128)(2,1)S(1)} %maximum_convert_fusion.own_ref), channel_id=1, source_target_pairs={{0,64},{32,96},{64,0},{96,32},{128,192},{160,224},{192,128},{224,1... | collective-permute-start | bytes 196616 | tf_op jit(solution)/shard_map/ppermute | solution.py:427
  97.4 5.0 %collective-permute-start.16 = (bf16[32,1024]{1,0:T(8,128)(2,1)S(1)}, bf16[32,1024]{1,0:T(8,128)(2,1)S(1)}, u32[]{:S(2)}, u32[]{:S(2)}) collective-permute-start(bf16[32,1024]{1,0:T(8,128)(2,1)S(1)} %maximum_convert_fusion.own_ref), channel_id=1, source_target_pairs={{0,96},{32,0},{64,32},{96,64},{128,224},{160,128},{192,160},{224,1... | collective-permute-start | bytes 196616 | tf_op jit(solution)/shard_map/ppermute | solution.py:427
  98.6 6.5 %collective-permute-start.18 = (bf16[128,1024]{1,0:T(8,128)(2,1)S(1)}, bf16[128,1024]{1,0:T(8,128)(2,1)S(1)}, u32[]{:S(2)}, u32[]{:S(2)}) collective-permute-start(bf16[128,1024]{1,0:T(8,128)(2,1)S(1)} %copy-done.5), channel_id=1, source_target_pairs={{0,1},{1,0},{2,3},{3,2},{4,5},{5,4},{6,7},{7,6},{8,9},{9,8},{10,11... | collective-permute-start | bytes 786440 | tf_op jit(solution)/shard_map/ppermute | solution.py:396
  103.7 1.8 %collective-permute-start.17 = (bf16[128,1024]{1,0:T(8,128)(2,1)}, bf16[128,1024]{1,0:T(8,128)(2,1)S(1)}, u32[]{:S(2)}, u32[]{:S(2)}) collective-permute-start(bf16[128,1024]{1,0:T(8,128)(2,1)} %gather_hidden.1.hid0_ref), channel_id=1, source_target_pairs={{0,1},{1,0},{2,3},{3,2},{4,5},{5,4},{6,7},{7,6},{8,9},{9,8},{10,11... | collective-permute-start | bytes 786440 | tf_op jit(solution)/shard_map/ppermute | solution.py:396
  103.7 1.4 %collective-permute-start.19 = (bf16[256,128]{1,0:T(8,128)(2,1)S(1)}, bf16[256,128]{1,0:T(8,128)(2,1)S(1)}, u32[]{:S(2)}, u32[]{:S(2)}) collective-permute-start(bf16[256,128]{1,0:T(8,128)(2,1)S(1)} %get-tuple-element.42), channel_id=1, source_target_pairs={{0,1},{1,0},{2,3},{3,2},{4,5},{5,4},{6,7},{7,6},{8,9},{9,8},{10,11... | collective-permute-start | bytes 196616 | tf_op jit(solution)/shard_map/ppermute | solution.py:396
  105.5 1.0 copy-start.2
  108.0 11.5 %collective-permute-start.20 = (bf16[128,1152]{1,0:T(8,128)(2,1)S(1)}, bf16[128,1152]{1,0:T(8,128)(2,1)S(1)}, u32[]{:S(2)}, u32[]{:S(2)}) collective-permute-start(bf16[128,1152]{1,0:T(8,128)(2,1)S(1)} %get-tuple-element.43), channel_id=1, source_target_pairs={{0,16},{1,17},{2,18},{3,19},{4,20},{5,21},{6,22},{7,23},{8,24},{9,... | collective-permute-start | bytes 884744 | tf_op jit(solution)/shard_map/ppermute | solution.py:434
  108.4 13.5 %collective-permute-start.21 = (bf16[128,1152]{1,0:T(8,128)(2,1)S(1)}, bf16[128,1152]{1,0:T(8,128)(2,1)S(1)}, u32[]{:S(2)}, u32[]{:S(2)}) collective-permute-start(bf16[128,1152]{1,0:T(8,128)(2,1)S(1)} %get-tuple-element.44), channel_id=1, source_target_pairs={{0,8},{1,9},{2,10},{3,11},{4,12},{5,13},{6,14},{7,15},{8,16},{9,17... | collective-permute-start | bytes 884744 | tf_op jit(solution)/shard_map/ppermute | solution.py:434
  110.3 14.6 %collective-permute-start.22 = (bf16[128,1152]{1,0:T(8,128)(2,1)S(1)}, bf16[128,1152]{1,0:T(8,128)(2,1)S(1)}, u32[]{:S(2)}, u32[]{:S(2)}) collective-permute-start(bf16[128,1152]{1,0:T(8,128)(2,1)S(1)} %get-tuple-element.45), channel_id=1, source_target_pairs={{0,24},{1,25},{2,26},{3,27},{4,28},{5,29},{6,30},{7,31},{8,0},{9,1... | collective-permute-start | bytes 884744 | tf_op jit(solution)/shard_map/ppermute | solution.py:434
  125.7 8.8 %collective-permute-start.23 = (bf16[32,1152]{1,0:T(8,128)(2,1)S(1)}, bf16[32,1152]{1,0:T(8,128)(2,1)S(1)}, u32[]{:S(2)}, u32[]{:S(2)}) collective-permute-start(bf16[32,1152]{1,0:T(8,128)(2,1)S(1)} %get-tuple-element.47), channel_id=1, source_target_pairs={{0,4},{1,5},{2,6},{3,7},{4,0},{5,1},{6,2},{7,3},{8,12},{9,13},{10,... | collective-permute-start | bytes 221192 | tf_op jit(solution)/shard_map/ppermute | solution.py:436
  130.6 6.6 %collective-permute-start.24 = (bf16[32,1152]{1,0:T(8,128)(2,1)S(1)}, bf16[32,1152]{1,0:T(8,128)(2,1)S(1)}, u32[]{:S(2)}, u32[]{:S(2)}) collective-permute-start(bf16[32,1152]{1,0:T(8,128)(2,1)S(1)} %get-tuple-element.48), channel_id=1, source_target_pairs={{0,2},{1,3},{2,4},{3,5},{4,6},{5,7},{6,0},{7,1},{8,10},{9,11},{10,... | collective-permute-start | bytes 221192 | tf_op jit(solution)/shard_map/ppermute | solution.py:436
  130.6 6.6 %collective-permute-start.25 = (bf16[32,1152]{1,0:T(8,128)(2,1)S(1)}, bf16[32,1152]{1,0:T(8,128)(2,1)S(1)}, u32[]{:S(2)}, u32[]{:S(2)}) collective-permute-start(bf16[32,1152]{1,0:T(8,128)(2,1)S(1)} %get-tuple-element.49), channel_id=1, source_target_pairs={{0,6},{1,7},{2,0},{3,1},{4,2},{5,3},{6,4},{7,5},{8,14},{9,15},{10,... | collective-permute-start | bytes 221192 | tf_op jit(solution)/shard_map/ppermute | solution.py:436
